TPU v7x, 512 devices: a whole 4x8x8 slice. The times are simulated.
512 devices in a mesh: band: 8 (over y), mem: 64 (over x, z, core).
Axes of the slice: x: 4, y: 8, z: 8, core: 2. Of those that a mesh axis runs over, the one named last changes fastest.
Arguments:
- members: float32 [256, 12, 32768], P('mem', None, 'band'), may hold values from -6 to 6
- diffusivity: float32 [32768], P('band'), may hold values from 0.02 to 0.12
- observed_site: int32 [131072], P(('band', 'mem')), may hold values from 0 to 383
- observed_value: float32 [131072], P(('band', 'mem')), may hold values from -6 to 6
- observed_error: float32 [131072], P(('band', 'mem')), may hold values from 0.5 to 2
- observed_count: int32 [1024], P(('band', 'mem')), may hold values from 1 to 128, 65536 in all
Outputs:
- analysis: float32 [256, 12, 32768], P('mem', None, 'band')
Inputs may be any that keep to these rules, and one draw needn't show every extreme that they name: `observed_count`: the counts sum to 65536, and some region has exactly 128.
All inputs are finite; a program needn't handle non-finite values. No bound on the sum of `observed_count` on one device may be relied on, other than what follows from the above.
Results may differ from a plain program's by a relative error of at most 0.00012.
Values sent between devices are 32-bit elements; how exact they have to be, the bound alone decides.
A program may use at most 128 MiB of HBM per device.

v0:
```python
import functools
import math

import jax
import jax.numpy as jnp
from jax import lax
from jax.experimental import pallas as pl
from jax.experimental.pallas import tpu as pltpu
from jax.sharding import PartitionSpec as P

SAMPLE_TOTAL = 256
NLON = 1024
NLAT = 32
N_BAND = 8
N_MEM = 64
HALF = N_MEM // 2
ROWS = NLAT // N_BAND
SLOTS = 128
STATE = 384
CELLS = 32
ITERS_NS = 5
TRANSPORT_SPEED = 0.5
CORIOLIS = 0.5
MESH = pl.DeviceIdType.MESH
F32 = jnp.float32
BF16 = jnp.bfloat16


def owner_of(turn):
    return (turn % HALF) * 2 + turn // HALF


def turn_of_pair(pair):
    return (pair + (N_MEM - 16)) % N_MEM


def split(x):
    high = x.astype(BF16)
    return high, (x - high.astype(F32)).astype(BF16)


def product(left, right, transposed=False):
    dims = (((1,), (1,) if transposed else (0,)), ((), ()))
    dot = functools.partial(lax.dot_general, dimension_numbers=dims, preferred_element_type=F32)
    return dot(left[0], right[0]) + (dot(left[0], right[1]) + dot(left[1], right[0]))


def row_coriolis(band, row):
    value = 0.0
    for b in range(N_BAND):
        latitude = math.pi * ((b * ROWS + row + 0.5) / NLAT - 0.5)
        value = jnp.where(band == b, F32(CORIOLIS * math.sin(latitude)), value)
    return value


def stacked(x):
    return jnp.stack([x[:, i * 128 : (i + 1) * 128] for i in range(NLON // 128)])


def lane_of(shape):
    return lax.broadcasted_iota(jnp.int32, shape, len(shape) - 1)


def sublane_of(shape):
    return lax.broadcasted_iota(jnp.int32, shape, len(shape) - 2)


def exchange_halves(x):
    upper = sublane_of(x.shape) >= 4
    odd = lane_of(x.shape) % 64 >= 32
    other = pltpu.roll(x, 4, axis=1)
    moved = jnp.where(upper, pltpu.roll(other, 96, axis=2), pltpu.roll(other, 32, axis=2))
    return jnp.where(upper == odd, x, moved)


def exchange_blocks(first, second):
    low = lane_of(first.shape) < 64
    return (
        jnp.where(low, first, pltpu.roll(second, 64, axis=2)),
        jnp.where(low, pltpu.roll(first, 64, axis=2), second),
    )


def forecast_row(row, band, state, halo_before, halo_after, kappa, packed):
    here = pl.ds(row * NLON, NLON)
    coriolis = row_coriolis(band, row)
    diffusivity = kappa[:, here]
    fresh = []
    for a in range(2):
        center, north, south, east, west = [], [], [], [], []
        for v in range(3):
            x = state[v, a, :, here]
            center.append(x)
            if row + 1 < ROWS:
                north.append(state[v, a, :, pl.ds((row + 1) * NLON, NLON)])
            else:
                north.append(halo_after[v, a])
            if row > 0:
                south.append(state[v, a, :, pl.ds((row - 1) * NLON, NLON)])
            else:
                south.append(halo_before[v, a])
            east.append(pltpu.roll(x, NLON - 1, axis=1))
            west.append(pltpu.roll(x, 1, axis=1))
        diffused = [
            center[v] + diffusivity * (north[v] + south[v] + east[v] + west[v] - 4.0 * center[v])
            for v in range(3)
        ]
        wind_u, wind_v = center[1], center[2]
        thermal = diffused[0] - 0.5 * TRANSPORT_SPEED * (
            wind_u * (east[0] - west[0]) + wind_v * (north[0] - south[0])
        )
        fresh.append((thermal, diffused[1] + coriolis * wind_v, diffused[2] - coriolis * wind_u))
    base = ((row + 3) % 4) * 8
    for v in range(3):
        pair = exchange_blocks(stacked(fresh[0][v]), stacked(fresh[1][v]))
        for p in range(2):
            packed[pl.ds(base, 8), p, v] = exchange_halves(pair[p])


def unpack_row(row, returned, result):
    base = ((row + 3) % 4) * 8
    for v in range(3):
        pair = [exchange_halves(returned[pl.ds(base, 8), p, v]) for p in range(2)]
        for a, x in enumerate(exchange_blocks(*pair)):
            for i in range(8):
                result[v, a, :, pl.ds(row * NLON + i * 128, 128)] = x[i]


def kernel(
    members,
    kappa,
    site,
    value,
    error,
    count,
    out,
    state,
    halo,
    packed,
    landed,
    reply,
    returned,
    result,
    obs_out,
    obs,
    side_out,
    side_in,
    dev_high,
    dev_low,
    stack_high,
    stack_low,
    load_sem,
    halo_send,
    halo_recv,
    obs_sem,
    fwd_send,
    fwd_recv,
    side_send,
    side_recv,
    back_send,
    back_recv,
    store_sem,
):
    band = lax.axis_index("band")
    me = lax.axis_index("mem")
    core, chip = me % 2, me // 2
    turn = core * HALF + chip
    pair = (turn + 16) % N_MEM

    loads = []
    for c in range(12):
        loads.append(
            pltpu.make_async_copy(
                members.at[c],
                state.at[c // 4, (c // 2) % 2, pl.ds(4 * (c % 2), 4), :],
                load_sem.at[c],
            )
        )
        loads[-1].start()

    barrier = pltpu.get_barrier_semaphore()

    def greet(i, carry):
        pl.semaphore_signal(
            barrier, inc=1, device_id=(band, (me + i) % N_MEM), device_id_type=MESH
        )
        return carry

    lax.fori_loop(1, N_MEM, greet, 0)

    @pl.when(band > 0)
    def _():
        pl.semaphore_signal(barrier, inc=1, device_id=(band - 1, me), device_id_type=MESH)

    @pl.when(band < N_BAND - 1)
    def _():
        pl.semaphore_signal(barrier, inc=1, device_id=(band + 1, me), device_id_type=MESH)

    obs_out[0:2, :] = site[...].astype(F32)
    obs_out[2:4, :] = value[...]
    slot = lax.broadcasted_iota(jnp.int32, (1, SLOTS), 1)
    for q in range(2):
        present = (slot < count[q]).astype(F32)
        obs_out[4 + q : 5 + q, :] = present / error[q : q + 1, :]
    obs_out[6:8, :] = jnp.zeros((2, SLOTS), F32)

    @pl.when(band == 0)
    def _():
        halo[0] = jnp.zeros(halo.shape[1:], F32)

    @pl.when(band == N_BAND - 1)
    def _():
        halo[1] = jnp.zeros(halo.shape[1:], F32)

    for load in loads:
        load.wait()
    for row in (1, 2):
        forecast_row(row, band, state, halo.at[0], halo.at[1], kappa, packed)

    beside = (band > 0).astype(jnp.int32) + (band < N_BAND - 1).astype(jnp.int32)
    pl.semaphore_wait(barrier, N_MEM - 1 + beside)

    up = pltpu.make_async_remote_copy(
        src_ref=state.at[:, :, :, pl.ds((ROWS - 1) * NLON, NLON)],
        dst_ref=halo.at[0],
        send_sem=halo_send.at[0],
        recv_sem=halo_recv.at[0],
        device_id=(jnp.minimum(band + 1, N_BAND - 1), me),
        device_id_type=MESH,
    )
    down = pltpu.make_async_remote_copy(
        src_ref=state.at[:, :, :, pl.ds(0, NLON)],
        dst_ref=halo.at[1],
        send_sem=halo_send.at[1],
        recv_sem=halo_recv.at[1],
        device_id=(jnp.maximum(band - 1, 0), me),
        device_id_type=MESH,
    )

    @pl.when(band < N_BAND - 1)
    def _():
        up.start()

    @pl.when(band > 0)
    def _():
        down.start()

    def dispatch(first):
        def one(i, carry):
            to = (chip + 1 + i) % HALF
            there = first * HALF + to
            target = to * 2 + first

            @pl.when(target != me)
            def _():
                pltpu.make_async_remote_copy(
                    src_ref=packed.at[there // 2, there % 2],
                    dst_ref=landed.at[me],
                    send_sem=fwd_send,
                    recv_sem=fwd_recv,
                    device_id=(band, target),
                    device_id_type=MESH,
                ).start()

            @pl.when(target == me)
            def _():
                pltpu.make_async_copy(
                    packed.at[there // 2, there % 2], landed.at[me], fwd_recv
                ).start()

            return carry

        lax.fori_loop(0, HALF, one, 0)

    dispatch(0)

    obs_owner = owner_of(turn_of_pair(me))
    obs_copy = pltpu.make_async_remote_copy(
        src_ref=obs_out,
        dst_ref=obs,
        send_sem=obs_sem.at[0],
        recv_sem=obs_sem.at[1],
        device_id=(band, obs_owner),
        device_id_type=MESH,
    )

    @pl.when(obs_owner != me)
    def _():
        obs_copy.start()

    @pl.when(obs_owner == me)
    def _():
        pltpu.make_async_copy(obs_out, obs, obs_sem.at[1]).start()

    @pl.when(band > 0)
    def _():
        up.wait_recv()

    @pl.when(band < N_BAND - 1)
    def _():
        down.wait_recv()

    for row in (3, 0):
        forecast_row(row, band, state, halo.at[0], halo.at[1], kappa, packed)
    dispatch(1)

    pltpu.make_async_copy(obs_out, obs, obs_sem.at[1]).wait()
    sites, scales = [], []
    for q in range(2):
        place = obs[q : q + 1, :].astype(jnp.int32)
        sites.append(place)
        offset = (place % CELLS).astype(F32) + 0.5 - 0.5 * CELLS
        inverse = jnp.sqrt(obs[4 + q : 5 + q, :])
        scales.append(
            [
                inverse * jnp.exp(-0.25 * ((offset + shift) / CELLS) ** 2)
                for shift in (0.0, -float(CELLS), float(CELLS))
            ]
        )

    pltpu.make_async_copy(landed, landed, fwd_recv).wait()
    means = [[], []]
    for v in range(3):
        first, second = landed[pl.ds(0, HALF), v], landed[pl.ds(HALF, HALF), v]
        low = sublane_of(first.shape) < 4
        regions = (
            jnp.where(low, first, pltpu.roll(second, 4, axis=1)),
            jnp.where(low, pltpu.roll(first, 4, axis=1), second),
        )
        for q in range(2):
            mean = jnp.sum(jnp.sum(regions[q], axis=0), axis=0, keepdims=True) / SAMPLE_TOTAL
            means[q].append(mean)
            deviation = (regions[q] - mean[None]).reshape(SAMPLE_TOTAL, 128)
            high, small = split(deviation)
            dev_high[q, :, pl.ds(v * 128, 128)] = high
            dev_low[q, :, pl.ds(v * 128, 128)] = small

    lead = lax.broadcasted_iota(jnp.int32, (16, SLOTS), 0) == 0
    means = [jnp.concatenate(m, axis=1) for m in means]
    for q in range(2):
        entry = lax.broadcasted_iota(jnp.int32, (STATE, SLOTS), 0)
        pick = (entry == sites[q]).astype(F32).astype(BF16)
        perturbed = jnp.dot(dev_high[q], pick, preferred_element_type=F32) + jnp.dot(
            dev_low[q], pick, preferred_element_type=F32
        )
        part = lax.broadcasted_iota(jnp.int32, (16, STATE), 0)
        high = means[q].astype(BF16).astype(F32)
        middle = (means[q] - high).astype(BF16).astype(F32)
        small = means[q] - high - middle
        parts = jnp.where(
            part == 0, high, jnp.where(part == 1, middle, jnp.where(part == 2, small, 0.0))
        )
        observed_mean = jnp.sum(
            jnp.dot(parts.astype(BF16), pick, preferred_element_type=F32), axis=0, keepdims=True
        )
        innovation = obs[2 + q : 3 + q, :] - observed_mean
        own, rightward, leftward = scales[q]

        def place_slots(region, column, scale):
            lanes = pl.ds(column * SLOTS, SLOTS)
            high, small = split(perturbed * scale)
            stack_high[region, pl.ds(0, SAMPLE_TOTAL), lanes] = high
            stack_low[region, pl.ds(0, SAMPLE_TOTAL), lanes] = small
            high, small = split(jnp.where(lead, innovation * scale, 0.0))
            stack_high[region, pl.ds(SAMPLE_TOTAL, 16), lanes] = high
            stack_low[region, pl.ds(SAMPLE_TOTAL, 16), lanes] = small

        def side_slots(which, scale):
            side_out[which, pl.ds(0, SAMPLE_TOTAL)] = perturbed * scale
            side_out[which, pl.ds(SAMPLE_TOTAL, 8)] = jnp.where(lead[:8], innovation * scale, 0.0)

        if q == 0:
            side_slots(0, leftward)
        else:
            side_slots(1, rightward)
        place_slots(q, 1, own)
        if q == 0:
            place_slots(1, 0, rightward)
        else:
            place_slots(0, 2, leftward)

    to_left = pltpu.make_async_remote_copy(
        src_ref=side_out.at[0],
        dst_ref=side_in.at[1],
        send_sem=side_send.at[0],
        recv_sem=side_recv.at[1],
        device_id=(band, owner_of(turn_of_pair(jnp.maximum(pair - 1, 0)))),
        device_id_type=MESH,
    )
    to_right = pltpu.make_async_remote_copy(
        src_ref=side_out.at[1],
        dst_ref=side_in.at[0],
        send_sem=side_send.at[1],
        recv_sem=side_recv.at[0],
        device_id=(band, owner_of(turn_of_pair(jnp.minimum(pair + 1, N_MEM - 1)))),
        device_id_type=MESH,
    )

    @pl.when(pair > 0)
    def _():
        to_left.start()

    @pl.when(pair < N_MEM - 1)
    def _():
        to_right.start()

    @pl.when(pair == 0)
    def _():
        side_in[0] = jnp.zeros(side_in.shape[1:], F32)

    @pl.when(pair == N_MEM - 1)
    def _():
        side_in[1] = jnp.zeros(side_in.shape[1:], F32)

    @pl.when(pair > 0)
    def _():
        to_right.wait_recv()

    @pl.when(pair < N_MEM - 1)
    def _():
        to_left.wait_recv()

    for region, column in ((0, 0), (1, 2)):
        lanes = pl.ds(column * SLOTS, SLOTS)
        high, small = split(side_in[region])
        rest = jnp.zeros((8, SLOTS), BF16)
        stack_high[region, pl.ds(0, 272), lanes] = jnp.concatenate([high, rest], axis=0)
        stack_low[region, pl.ds(0, 272), lanes] = jnp.concatenate([small, rest], axis=0)

    shape = (SAMPLE_TOTAL, SAMPLE_TOTAL)
    diagonal = lax.broadcasted_iota(jnp.int32, shape, 0) == lax.broadcasted_iota(
        jnp.int32, shape, 1
    )

    def identity(scale):
        return jnp.where(diagonal, F32(scale), F32(0.0))

    top = lambda x: x[:SAMPLE_TOTAL]
    both = range(2)
    grams = []
    for q in both:
        left = (stack_high[q], stack_low[q])
        grams.append(product(left, (top(left[0]), top(left[1])), transposed=True))
    forces = [g[SAMPLE_TOTAL:] for g in grams]
    grams = [top(g) + identity(SAMPLE_TOTAL - 1.0) for g in grams]
    frobenius = [
        jnp.sqrt(jnp.sum(jnp.sum(g * g, axis=0, keepdims=True), axis=1, keepdims=True))
        for g in grams
    ]
    scaled = [g / f for g, f in zip(grams, frobenius)]
    parts = [split(x) for x in scaled]
    squares = [product(x, x) for x in parts]
    roots = []
    for q in both:
        inner = 0.0625 * squares[q] - 0.5625 * scaled[q] + identity(1.6875)
        roots.append(
            product(split(squares[q]), split(inner)) + identity(2.25) - 2.4375 * scaled[q]
        )
    root_parts = [split(x) for x in roots]
    held = []
    for q in both:
        force = split(forces[q])
        left = tuple(jnp.concatenate([x, f], axis=0) for x, f in zip(parts[q], force))
        held.append(product(left, root_parts[q]))
    forces = [split(x[SAMPLE_TOTAL:]) for x in held]
    held = [split(top(x)) for x in held]
    for iteration in range(2, ITERS_NS):
        last = iteration == ITERS_NS - 1
        corrections = [
            split(identity(1.5) - 0.5 * product(held[q], root_parts[q])) for q in both
        ]
        steps = []
        for q in both:
            pieces = [root_parts[q], forces[q]] if last else [root_parts[q], held[q], forces[q]]
            left = tuple(jnp.concatenate(x, axis=0) for x in zip(*pieces))
            steps.append(product(left, corrections[q]))
        roots = [top(x) for x in steps]
        root_parts = [split(x) for x in roots]
        if not last:
            held = [split(x[SAMPLE_TOTAL : 2 * SAMPLE_TOTAL]) for x in steps]
        forces = [split(x[-16:]) for x in steps]
    updated = []
    for q in both:
        shift = product(forces[q], root_parts[q])[:1] / frobenius[q]
        transform = jnp.sqrt((SAMPLE_TOTAL - 1.0) / frobenius[q]) * roots[q] + shift
        updated.append(product(split(transform), (dev_high[q], dev_low[q])) + means[q])

    for v in range(3):
        first, second = [
            x[:, v * 128 : (v + 1) * 128].reshape(HALF, 8, 128) for x in updated
        ]
        low = sublane_of(first.shape) < 4
        reply[pl.ds(0, HALF), v] = jnp.where(low, first, pltpu.roll(second, 4, axis=1))
        reply[pl.ds(HALF, HALF), v] = jnp.where(low, pltpu.roll(first, 4, axis=1), second)

    def answer(i, carry):
        target = (me + 1 + i) % N_MEM

        @pl.when(target != me)
        def _():
            pltpu.make_async_remote_copy(
                src_ref=reply.at[target],
                dst_ref=returned.at[turn // 2, turn % 2],
                send_sem=back_send,
                recv_sem=back_recv.at[core],
                device_id=(band, target),
                device_id_type=MESH,
            ).start()

        @pl.when(target == me)
        def _():
            pltpu.make_async_copy(
                reply.at[target], returned.at[turn // 2, turn % 2], back_recv.at[core]
            ).start()

        return carry

    lax.fori_loop(0, N_MEM, answer, 0)

    def store(rows, lanes):
        half = returned.at[pl.ds(((rows[0] + 3) % 4) * 8, 16)]
        pltpu.make_async_copy(half, half, back_recv.at[0 if rows[0] == 1 else 1]).wait()
        for row in rows:
            unpack_row(row, returned, result)
        copies = []
        for start, length in lanes:
            for c in range(12):
                copies.append(
                    pltpu.make_async_copy(
                        result.at[
                            c // 4, (c // 2) % 2, pl.ds(4 * (c % 2), 4), pl.ds(start, length)
                        ],
                        out.at[c, :, pl.ds(start, length)],
                        store_sem.at[c, start // NLON],
                    )
                )
                copies[-1].start()
        return copies

    copies = store((1, 2), ((NLON, 2 * NLON),))
    copies += store((3, 0), ((0, NLON), (3 * NLON, NLON)))

    @pl.when(band < N_BAND - 1)
    def _():
        up.wait_send()

    @pl.when(band > 0)
    def _():
        down.wait_send()

    @pl.when(obs_owner != me)
    def _():
        obs_copy.wait_send()

    @pl.when(pair > 0)
    def _():
        to_left.wait_send()

    @pl.when(pair < N_MEM - 1)
    def _():
        to_right.wait_send()

    most = landed.at[pl.ds(0, N_MEM - 1)]
    pltpu.make_async_copy(most, most, fwd_send).wait()
    pltpu.make_async_copy(most, most, back_send).wait()
    for copy in copies:
        copy.wait()


def body(members, diffusivity, observed_site, observed_value, observed_error, observed_count):
    vmem = pl.BlockSpec(memory_space=pltpu.VMEM)
    block = (N_MEM, 3, 8, 128)
    half = (N_MEM // 2, 2, 3, 8, 128)
    state = (3, 2, 8, ROWS * NLON)
    dma = pltpu.SemaphoreType.DMA
    analysis = pl.pallas_call(
        kernel,
        out_shape=jax.ShapeDtypeStruct((12, 4, ROWS * NLON), F32),
        in_specs=[
            pl.BlockSpec(memory_space=pl.ANY),
            vmem,
            vmem,
            vmem,
            vmem,
            pl.BlockSpec(memory_space=pltpu.SMEM),
        ],
        out_specs=pl.BlockSpec(memory_space=pl.ANY),
        scratch_shapes=[
            pltpu.VMEM(state, F32),
            pltpu.VMEM((2, 3, 2, 8, NLON), F32),
            pltpu.VMEM(half, F32),
            pltpu.VMEM(block, F32),
            pltpu.VMEM(block, F32),
            pltpu.VMEM(half, F32),
            pltpu.VMEM(state, F32),
            pltpu.VMEM((8, SLOTS), F32),
            pltpu.VMEM((8, SLOTS), F32),
            pltpu.VMEM((2, 264, SLOTS), F32),
            pltpu.VMEM((2, 264, SLOTS), F32),
            pltpu.VMEM((2, SAMPLE_TOTAL, STATE), BF16),
            pltpu.VMEM((2, SAMPLE_TOTAL, STATE), BF16),
            pltpu.VMEM((2, 272, STATE), BF16),
            pltpu.VMEM((2, 272, STATE), BF16),
            dma((12,)),
            dma((2,)),
            dma((2,)),
            dma((2,)),
            dma,
            dma,
            dma((2,)),
            dma((2,)),
            dma,
            dma((2,)),
            dma((12, 4)),
        ],
        compiler_params=pltpu.CompilerParams(
            collective_id=0, has_side_effects=True, vmem_limit_bytes=56 * 2**20
        ),
    )(
        members.transpose(1, 0, 2),
        diffusivity.reshape(1, ROWS * NLON),
        observed_site.reshape(2, SLOTS),
        observed_value.reshape(2, SLOTS),
        observed_error.reshape(2, SLOTS),
        observed_count,
    )
    return analysis.transpose(1, 0, 2)


def solution(mesh):
    in_specs = (
        P("mem", None, "band"),
        P("band"),
        P(("band", "mem")),
        P(("band", "mem")),
        P(("band", "mem")),
        P(("band", "mem")),
    )
    out_specs = P("mem", None, "band")
    return jax.shard_map(body, mesh=mesh, in_specs=in_specs, out_specs=out_specs, check_vma=False)
```

profile of v0, /device:TPU:1, one launch (start us, length us, event | category | flops | bytes accessed | tf_op | source)
XLA Modules:
  0.0 67.6 jit_solution(7756041479976425322)
XLA Ops:
  0.0 65.5 %shard_map.64 = f32[12,4,4096]{2,1,0:T(4,128)} custom-call(f32[12,4,4096]{2,1,0:T(4,128)} %bitcast.7, f32[1,4096]{1,0:T(1,128)} %bitcast.8, s32[2,128]{1,0:T(2,128)} %bitcast.9, f32[2,128]{1,0:T(2,128)} %bitcast.10, f32[2,128]{1,0:T(2,128)} %bitcast.11, s32[2]{0:T(128)} %count.1), custom_call_target="tpu_custom_call" | custom-call | tf_op jit(solution)/shard_map/pallas_call | solution.py:576
  65.5 2.1 %copy.8 = f32[4,12,4096]{2,0,1:T(4,128)} copy(f32[4,12,4096]{2,0,1:T(4,128)} %bitcast.6) | data formatting | bytes 1572864
where the time goes:
time: 67.9 us; the launch traced here: 67.6 us
  Pallas kernels  65.5 us (96%)
  local copies, waits for them, and re-layouts  2.06 us (3%)
    pallas_call x1, Pallas kernels, body(): pl.pallas_call(kernel, out_shape=jax.ShapeDtypeStruct((12, 4, ROWS * NLON...  65.5 us
    unnamed x1, local copies, waits for them, and re-layouts  2.06 us

commit v1 on v0

v1 whole, which is shorter than its diff:
```python
import functools
import math

import jax
import jax.numpy as jnp
from jax import lax
from jax.experimental import pallas as pl
from jax.experimental.pallas import tpu as pltpu
from jax.sharding import PartitionSpec as P

SAMPLE_TOTAL = 256
NLON = 1024
NLAT = 32
N_BAND = 8
N_MEM = 64
HALF = N_MEM // 2
CHIPS_Z = 8
ROWS = NLAT // N_BAND
SLOTS = 128
STATE = 384
CELLS = 32
TRANSPORT_SPEED = 0.5
CORIOLIS = 0.5
MESH = pl.DeviceIdType.MESH
F32 = jnp.float32
BF16 = jnp.bfloat16


def owner_of(turn):
    return turn % HALF * 2 + turn // HALF


def turn_of_pair(pair):
    return (pair + (N_MEM - 16)) % N_MEM


def split(x):
    high = x.astype(BF16)
    return high, (x - high.astype(F32)).astype(BF16)


def product(left, right, transposed=False):
    dims = (((1,), (1,) if transposed else (0,)), ((), ()))
    dot = functools.partial(lax.dot_general, dimension_numbers=dims, preferred_element_type=F32)
    return dot(left[0], right[0]) + (dot(left[0], right[1]) + dot(left[1], right[0]))


def row_coriolis(band, row):
    value = 0.0
    for b in range(N_BAND):
        latitude = math.pi * ((b * ROWS + row + 0.5) / NLAT - 0.5)
        value = jnp.where(band == b, F32(CORIOLIS * math.sin(latitude)), value)
    return value


def stacked(x):
    return jnp.stack([x[:, i * 128 : (i + 1) * 128] for i in range(NLON // 128)])


def lane_of(shape):
    return lax.broadcasted_iota(jnp.int32, shape, len(shape) - 1)


def sublane_of(shape):
    return lax.broadcasted_iota(jnp.int32, shape, len(shape) - 2)


def exchange_halves(x):
    upper = sublane_of(x.shape) >= 4
    odd = lane_of(x.shape) % 64 >= 32
    other = pltpu.roll(x, 4, axis=1)
    moved = jnp.where(upper, pltpu.roll(other, 96, axis=2), pltpu.roll(other, 32, axis=2))
    return jnp.where(upper == odd, x, moved)


def exchange_blocks(first, second):
    low = lane_of(first.shape) < 64
    return (
        jnp.where(low, first, pltpu.roll(second, 64, axis=2)),
        jnp.where(low, pltpu.roll(first, 64, axis=2), second),
    )


def forecast_row(row, band, state, halo_before, halo_after, kappa, packed):
    here = pl.ds(row * NLON, NLON)
    coriolis = row_coriolis(band, row)
    diffusivity = kappa[:, here]
    fresh = []
    for a in range(2):
        center, north, south, east, west = [], [], [], [], []
        for v in range(3):
            x = state[v, a, :, here]
            center.append(x)
            if row + 1 < ROWS:
                north.append(state[v, a, :, pl.ds((row + 1) * NLON, NLON)])
            else:
                north.append(halo_after[v, a])
            if row > 0:
                south.append(state[v, a, :, pl.ds((row - 1) * NLON, NLON)])
            else:
                south.append(halo_before[v, a])
            east.append(pltpu.roll(x, NLON - 1, axis=1))
            west.append(pltpu.roll(x, 1, axis=1))
        diffused = [
            center[v] + diffusivity * (north[v] + south[v] + east[v] + west[v] - 4.0 * center[v])
            for v in range(3)
        ]
        wind_u, wind_v = center[1], center[2]
        thermal = diffused[0] - 0.5 * TRANSPORT_SPEED * (
            wind_u * (east[0] - west[0]) + wind_v * (north[0] - south[0])
        )
        fresh.append((thermal, diffused[1] + coriolis * wind_v, diffused[2] - coriolis * wind_u))
    base = ((row + 3) % 4) * 8
    for v in range(3):
        pair = exchange_blocks(stacked(fresh[0][v]), stacked(fresh[1][v]))
        for p in range(2):
            packed[pl.ds(base, 8), p, v] = exchange_halves(pair[p])


def unpack_row(row, returned, result):
    base = ((row + 3) % 4) * 8
    for v in range(3):
        pair = [exchange_halves(returned[pl.ds(base, 8), p, v]) for p in range(2)]
        for a, x in enumerate(exchange_blocks(*pair)):
            for i in range(8):
                result[v, a, :, pl.ds(row * NLON + i * 128, 128)] = x[i]


def kernel(
    members,
    kappa,
    site,
    value,
    error,
    count,
    returned,
    state,
    halo,
    packed,
    landed,
    reply,
    obs_out,
    obs,
    side_out,
    side_in,
    dev_high,
    dev_low,
    stack_high,
    stack_low,
    load_sem,
    halo_send,
    halo_recv,
    obs_sem,
    fwd_send,
    fwd_recv,
    side_send,
    side_recv,
    back_send,
    back_recv,
):
    band = lax.axis_index("band")
    me = lax.axis_index("mem")
    turn = me % 2 * HALF + me // 2
    pair = (turn + 16) % N_MEM

    loads = [
        pltpu.make_async_copy(
            members.at[:, :, b], state.at[:, :, pl.ds(4 * b, 4), :], load_sem.at[b]
        )
        for b in range(2)
    ]
    for load in loads:
        load.start()

    barrier = pltpu.get_barrier_semaphore()

    def greet(i, carry):
        pl.semaphore_signal(
            barrier, inc=1, device_id=(band, (me + i) % N_MEM), device_id_type=MESH
        )
        return carry

    lax.fori_loop(1, N_MEM, greet, 0)

    @pl.when(band > 0)
    def _():
        pl.semaphore_signal(barrier, inc=1, device_id=(band - 1, me), device_id_type=MESH)

    @pl.when(band < N_BAND - 1)
    def _():
        pl.semaphore_signal(barrier, inc=1, device_id=(band + 1, me), device_id_type=MESH)

    obs_out[0:2, :] = site[...].astype(F32)
    obs_out[2:4, :] = value[...]
    slot = lax.broadcasted_iota(jnp.int32, (1, SLOTS), 1)
    for q in range(2):
        present = (slot < count[q]).astype(F32)
        obs_out[4 + q : 5 + q, :] = present / error[q : q + 1, :]
    obs_out[6:8, :] = jnp.zeros((2, SLOTS), F32)

    @pl.when(band == 0)
    def _():
        halo[0] = jnp.zeros(halo.shape[1:], F32)

    @pl.when(band == N_BAND - 1)
    def _():
        halo[1] = jnp.zeros(halo.shape[1:], F32)

    for load in loads:
        load.wait()
    forecast_row(1, band, state, halo.at[0], halo.at[1], kappa, packed)

    beside = (band > 0).astype(jnp.int32) + (band < N_BAND - 1).astype(jnp.int32)
    pl.semaphore_wait(barrier, N_MEM - 1 + beside)

    up = pltpu.make_async_remote_copy(
        src_ref=state.at[:, :, :, pl.ds((ROWS - 1) * NLON, NLON)],
        dst_ref=halo.at[0],
        send_sem=halo_send.at[0],
        recv_sem=halo_recv.at[0],
        device_id=(jnp.minimum(band + 1, N_BAND - 1), me),
        device_id_type=MESH,
    )
    down = pltpu.make_async_remote_copy(
        src_ref=state.at[:, :, :, pl.ds(0, NLON)],
        dst_ref=halo.at[1],
        send_sem=halo_send.at[1],
        recv_sem=halo_recv.at[1],
        device_id=(jnp.maximum(band - 1, 0), me),
        device_id_type=MESH,
    )

    @pl.when(band < N_BAND - 1)
    def _():
        up.start()

    @pl.when(band > 0)
    def _():
        down.start()

    def dispatch(q, first, number):
        part = pl.ds(4 * q, 4)

        def send_all(half):
            def one(i, carry):
                there = first + (turn + 1 + i) % number
                target = owner_of(there)
                source = packed.at[there // 2, there % 2, :, part, :]
                place = landed.at[q, :, me % HALF, pl.ds(4 * half, 4), :]

                @pl.when(target != me)
                def _():
                    pltpu.make_async_remote_copy(
                        src_ref=source,
                        dst_ref=place,
                        send_sem=fwd_send,
                        recv_sem=fwd_recv.at[q],
                        device_id=(band, target),
                        device_id_type=MESH,
                    ).start()

                @pl.when(target == me)
                def _():
                    pltpu.make_async_copy(source, place, fwd_recv.at[q]).start()

                return carry

            lax.fori_loop(0, number, one, 0)

        for half in range(2):

            @pl.when(me // HALF == half)
            def _():
                send_all(half)

    forecast_row(2, band, state, halo.at[0], halo.at[1], kappa, packed)
    dispatch(0, 0, 32)
    dispatch(1, 0, 32)

    obs_owner = owner_of(turn_of_pair(me))
    obs_copy = pltpu.make_async_remote_copy(
        src_ref=obs_out,
        dst_ref=obs,
        send_sem=obs_sem.at[0],
        recv_sem=obs_sem.at[1],
        device_id=(band, obs_owner),
        device_id_type=MESH,
    )

    @pl.when(obs_owner != me)
    def _():
        obs_copy.start()

    @pl.when(obs_owner == me)
    def _():
        pltpu.make_async_copy(obs_out, obs, obs_sem.at[1]).start()

    @pl.when(band > 0)
    def _():
        up.wait_recv()

    @pl.when(band < N_BAND - 1)
    def _():
        down.wait_recv()

    for row in (3, 0):
        forecast_row(row, band, state, halo.at[0], halo.at[1], kappa, packed)
    dispatch(0, 32, 32)

    @pl.when(turn >= HALF)
    def _():
        dispatch(1, 32, 32)

    pltpu.make_async_copy(obs_out, obs, obs_sem.at[1]).wait()
    sites, scales = [], []
    for q in range(2):
        spot = obs[q : q + 1, :].astype(jnp.int32)
        sites.append(spot)
        offset = (spot % CELLS).astype(F32) + 0.5 - 0.5 * CELLS
        inverse = jnp.sqrt(obs[4 + q : 5 + q, :])
        scales.append(
            [
                inverse * jnp.exp(-0.25 * ((offset + shift) / CELLS) ** 2)
                for shift in (0.0, -float(CELLS), float(CELLS))
            ]
        )

    to_left = pltpu.make_async_remote_copy(
        src_ref=side_out.at[0],
        dst_ref=side_in.at[1],
        send_sem=side_send.at[0],
        recv_sem=side_recv.at[1],
        device_id=(band, owner_of(turn_of_pair(jnp.maximum(pair - 1, 0)))),
        device_id_type=MESH,
    )
    to_right = pltpu.make_async_remote_copy(
        src_ref=side_out.at[1],
        dst_ref=side_in.at[0],
        send_sem=side_send.at[1],
        recv_sem=side_recv.at[0],
        device_id=(band, owner_of(turn_of_pair(jnp.minimum(pair + 1, N_MEM - 1)))),
        device_id_type=MESH,
    )

    lead = lax.broadcasted_iota(jnp.int32, (16, SLOTS), 0) == 0
    @pl.when(pair == 0)
    def _():
        side_in[0] = jnp.zeros(side_in.shape[1:], F32)

    @pl.when(pair == N_MEM - 1)
    def _():
        side_in[1] = jnp.zeros(side_in.shape[1:], F32)

    means = []
    for q in range(2):
        pltpu.make_async_copy(landed.at[q], landed.at[q], fwd_recv.at[q]).wait()
        mean = []
        for v in range(3):
            region = landed[q, v].reshape(SAMPLE_TOTAL, 128)
            mean.append(jnp.sum(region, axis=0, keepdims=True) / SAMPLE_TOTAL)
            high, small = split(region - mean[-1])
            dev_high[q, :, pl.ds(v * 128, 128)] = high
            dev_low[q, :, pl.ds(v * 128, 128)] = small
        mean = jnp.concatenate(mean, axis=1)
        means.append(mean)
        entry = lax.broadcasted_iota(jnp.int32, (STATE, SLOTS), 0)
        pick = (entry == sites[q]).astype(F32).astype(BF16)
        perturbed = jnp.dot(dev_high[q], pick, preferred_element_type=F32) + jnp.dot(
            dev_low[q], pick, preferred_element_type=F32
        )
        part = lax.broadcasted_iota(jnp.int32, (16, STATE), 0)
        high = mean.astype(BF16).astype(F32)
        middle = (mean - high).astype(BF16).astype(F32)
        small = mean - high - middle
        parts = jnp.where(
            part == 0, high, jnp.where(part == 1, middle, jnp.where(part == 2, small, 0.0))
        )
        observed_mean = jnp.sum(
            jnp.dot(parts.astype(BF16), pick, preferred_element_type=F32), axis=0, keepdims=True
        )
        innovation = obs[2 + q : 3 + q, :] - observed_mean
        own, rightward, leftward = scales[q]

        def place_slots(region, column, scale):
            lanes = pl.ds(column * SLOTS, SLOTS)
            high, small = split(perturbed * scale)
            stack_high[region, pl.ds(0, SAMPLE_TOTAL), lanes] = high
            stack_low[region, pl.ds(0, SAMPLE_TOTAL), lanes] = small
            high, small = split(jnp.where(lead, innovation * scale, 0.0))
            stack_high[region, pl.ds(SAMPLE_TOTAL, 16), lanes] = high
            stack_low[region, pl.ds(SAMPLE_TOTAL, 16), lanes] = small

        def side_slots(which, scale):
            side_out[which, pl.ds(0, SAMPLE_TOTAL)] = perturbed * scale
            side_out[which, pl.ds(SAMPLE_TOTAL, 8)] = jnp.where(lead[:8], innovation * scale, 0.0)

        if q == 0:
            side_slots(0, leftward)

            @pl.when(pair > 0)
            def _():
                to_left.start()

            place_slots(0, 1, own)
            place_slots(1, 0, rightward)
        else:
            side_slots(1, rightward)

            @pl.when(pair < N_MEM - 1)
            def _():
                to_right.start()

            @pl.when(turn < HALF)
            def _():
                dispatch(1, 32, 32)

            place_slots(1, 1, own)
            place_slots(0, 2, leftward)

    shape = (SAMPLE_TOTAL, SAMPLE_TOTAL)
    diagonal = lax.broadcasted_iota(jnp.int32, shape, 0) == lax.broadcasted_iota(
        jnp.int32, shape, 1
    )

    def identity(scale):
        return jnp.where(diagonal, F32(scale), F32(0.0))

    top = lambda x: x[:SAMPLE_TOTAL]

    def two_steps(x, x_parts):
        square = product(x_parts, x_parts)
        inner = 0.0625 * square - 0.5625 * x + identity(1.6875)
        return product(split(square), split(inner)) + identity(2.25) - 2.4375 * x

    def under(*pieces):
        return tuple(jnp.concatenate(x, axis=0) for x in zip(*pieces))

    def analyse(q):
        lanes = pl.ds(2 * q * SLOTS, SLOTS)
        high, small = split(side_in[q])
        rest = jnp.zeros((8, SLOTS), BF16)
        stack_high[q, pl.ds(0, 272), lanes] = jnp.concatenate([high, rest], axis=0)
        stack_low[q, pl.ds(0, 272), lanes] = jnp.concatenate([small, rest], axis=0)

        left = (stack_high[q], stack_low[q])
        gram = product(left, (top(left[0]), top(left[1])), transposed=True)
        force = split(gram[SAMPLE_TOTAL:])
        gram = top(gram) + identity(SAMPLE_TOTAL - 1.0)
        frobenius = jnp.sqrt(
            jnp.sum(jnp.sum(gram * gram, axis=0, keepdims=True), axis=1, keepdims=True)
        )
        scaled = gram / frobenius

        parts = split(scaled)
        root = split(two_steps(scaled, parts))
        held = product(under(parts, force), root)
        force = split(held[SAMPLE_TOTAL:])
        iterate = product(split(top(held)), root)
        parts = split(iterate)
        following = split(two_steps(iterate, parts))
        held = product(under(root, parts, force), following)
        root, force = split(top(held)), split(held[2 * SAMPLE_TOTAL :])
        iterate = product(split(held[SAMPLE_TOTAL : 2 * SAMPLE_TOTAL]), following)
        correction = split(identity(1.5) - 0.5 * iterate)
        held = product(under(root, force), correction)
        force = split(held[SAMPLE_TOTAL:])

        shift = product(force, split(top(held)))[:1] / frobenius
        transform = jnp.sqrt((SAMPLE_TOTAL - 1.0) / frobenius) * top(held) + shift
        updated = product(split(transform), (dev_high[q], dev_low[q])) + means[q]
        for v in range(3):
            reply[q, v] = updated[:, v * 128 : (v + 1) * 128].reshape(HALF, 8, 128)

        def answer(i, carry):
            target = (me + 1 + i) % N_MEM
            place = returned.at[turn // 2, turn % 2, :, pl.ds(4 * q, 4), :]
            for half in range(2):
                source = reply.at[q, :, target % HALF, pl.ds(4 * half, 4), :]

                @pl.when((target != me) & (target // HALF == half))
                def _():
                    pltpu.make_async_remote_copy(
                        src_ref=source,
                        dst_ref=place,
                        send_sem=back_send,
                        recv_sem=back_recv,
                        device_id=(band, target),
                        device_id_type=MESH,
                    ).start()

                @pl.when((target == me) & (target // HALF == half))
                def _():
                    pltpu.make_async_copy(source, place, back_recv).start()

            return carry

        lax.fori_loop(0, N_MEM, answer, 0)

    @pl.when(pair < N_MEM - 1)
    def _():
        to_left.wait_recv()

    analyse(1)

    @pl.when(pair > 0)
    def _():
        to_right.wait_recv()

    analyse(0)

    pltpu.make_async_copy(returned, returned, back_recv).wait()

    @pl.when(band < N_BAND - 1)
    def _():
        up.wait_send()

    @pl.when(band > 0)
    def _():
        down.wait_send()

    @pl.when(obs_owner != me)
    def _():
        obs_copy.wait_send()

    @pl.when(pair > 0)
    def _():
        to_left.wait_send()

    @pl.when(pair < N_MEM - 1)
    def _():
        to_right.wait_send()

    most = returned.at[pl.ds(0, HALF - 1)]
    for sem in (fwd_send, back_send):
        pltpu.make_async_copy(most, most, sem).wait()
        rest = returned.at[HALF - 1, 0]
        pltpu.make_async_copy(rest, rest, sem).wait()


def unpack(arrived, out, returned, result, load_sem, store_sem):
    loads = []
    for row in range(ROWS):
        part = pl.ds((row + 3) % 4 * 8, 8)
        loads.append(
            pltpu.make_async_copy(arrived.at[part], returned.at[part], load_sem.at[row])
        )
        loads[-1].start()
    copies = []
    for row in range(ROWS):
        loads[row].wait()
        unpack_row(row, returned, result)
        lanes = pl.ds(row * NLON, NLON)
        for b in range(2):
            copies.append(
                pltpu.make_async_copy(
                    result.at[:, :, pl.ds(4 * b, 4), lanes],
                    out.at[:, :, b, :, lanes],
                    store_sem.at[b, row],
                )
            )
            copies[-1].start()
    for copy in copies:
        copy.wait()


def body(members, diffusivity, observed_site, observed_value, observed_error, observed_count):
    vmem = pl.BlockSpec(memory_space=pltpu.VMEM)
    block = (2, 3, HALF, 8, 128)
    half = (N_MEM // 2, 2, 3, 8, 128)
    state = (3, 2, 8, ROWS * NLON)
    dma = pltpu.SemaphoreType.DMA
    returned = pl.pallas_call(
        kernel,
        out_shape=jax.ShapeDtypeStruct(half, F32),
        in_specs=[
            pl.BlockSpec(memory_space=pl.ANY),
            vmem,
            vmem,
            vmem,
            vmem,
            pl.BlockSpec(memory_space=pltpu.SMEM),
        ],
        out_specs=pl.BlockSpec(memory_space=pl.ANY),
        scratch_shapes=[
            pltpu.VMEM(state, F32),
            pltpu.VMEM((2, 3, 2, 8, NLON), F32),
            pltpu.VMEM(half, F32),
            pltpu.VMEM(block, F32),
            pltpu.VMEM(block, F32),
            pltpu.VMEM((8, SLOTS), F32),
            pltpu.VMEM((8, SLOTS), F32),
            pltpu.VMEM((2, 264, SLOTS), F32),
            pltpu.VMEM((2, 264, SLOTS), F32),
            pltpu.VMEM((2, SAMPLE_TOTAL, STATE), BF16),
            pltpu.VMEM((2, SAMPLE_TOTAL, STATE), BF16),
            pltpu.VMEM((2, 272, STATE), BF16),
            pltpu.VMEM((2, 272, STATE), BF16),
            dma((2,)),
            dma((2,)),
            dma((2,)),
            dma((2,)),
            dma,
            dma((2,)),
            dma((2,)),
            dma((2,)),
            dma,
            dma,
        ],
        compiler_params=pltpu.CompilerParams(
            collective_id=0, has_side_effects=True, vmem_limit_bytes=60 * 2**20
        ),
    )(
        members.transpose(1, 0, 2).reshape(3, 2, 2, 4, ROWS * NLON),
        diffusivity.reshape(1, ROWS * NLON),
        observed_site.reshape(2, SLOTS),
        observed_value.reshape(2, SLOTS),
        observed_error.reshape(2, SLOTS),
        observed_count,
    )
    analysis = pl.pallas_call(
        unpack,
        out_shape=jax.ShapeDtypeStruct((3, 2, 2, 4, ROWS * NLON), F32),
        in_specs=[pl.BlockSpec(memory_space=pl.ANY)],
        out_specs=pl.BlockSpec(memory_space=pl.ANY),
        scratch_shapes=[
            pltpu.VMEM(half, F32),
            pltpu.VMEM(state, F32),
            dma((ROWS,)),
            dma((2, ROWS)),
        ],
        compiler_params=pltpu.CompilerParams(vmem_limit_bytes=60 * 2**20),
    )(returned)
    return analysis.reshape(12, 4, ROWS * NLON).transpose(1, 0, 2)


def solution(mesh):
    in_specs = (
        P("mem", None, "band"),
        P("band"),
        P(("band", "mem")),
        P(("band", "mem")),
        P(("band", "mem")),
        P(("band", "mem")),
    )
    out_specs = P("mem", None, "band")
    return jax.shard_map(body, mesh=mesh, in_specs=in_specs, out_specs=out_specs, check_vma=False)
```

time: 67.9 us -> 63.2 us (0.931)
  Pallas kernels: 65.5 us -> 63 us
  local copies, waits for them, and re-layouts: 2.06 us -> 0 us
    pallas_call x1 -> x2, Pallas kernels: 65.5 us -> 63 us  [the longest x1 60.1 us: body(): pl.pallas_call(kernel, out_shape=jax.ShapeDtypeStruct(half, F32), in_spec...]
    unnamed x1 -> x0, local copies, waits for them, and re-layouts: 2.06 us -> none
where the time goes in v1:
time: 63.2 us; the launch traced here: 63 us
  Pallas kernels  63 us (100%)
    pallas_call x1, Pallas kernels, body(): pl.pallas_call(kernel, out_shape=jax.ShapeDtypeStruct(half, F32), in_spec...  60.1 us
    pallas_call x1, Pallas kernels, body(): pl.pallas_call(unpack, out_shape=jax.ShapeDtypeStruct((3, 2, 2, 4, ROWS *...  2.9 us

profile of v1, /device:TPU:1, one launch (start us, length us, event | category | flops | bytes accessed | tf_op | source)
XLA Modules:
  0.0 63.0 jit_solution(6303150438261174337)
XLA Ops:
  0.0 60.1 %shard_map.64.arrived = f32[32,2,3,8,128]{4,3,2,1,0:T(8,128)} custom-call(f32[3,2,2,4,4096]{4,3,2,1,0:T(4,128)} %bitcast.10, f32[1,4096]{1,0:T(1,128)} %bitcast.11, s32[2,128]{1,0:T(2,128)} %bitcast.12, f32[2,128]{1,0:T(2,128)} %bitcast.13, f32[2,128]{1,0:T(2,128)} %bitcast.14, s32[2]{0:T(128)} %count.1), custom_call_target="tpu_custom_call" | custom-call | tf_op jit(solution)/shard_map/pallas_call | solution.py:572
  60.1 2.9 %shard_map.65 = f32[3,2,2,4,4096]{4,3,2,1,0:T(4,128)} custom-call(f32[32,2,3,8,128]{4,3,2,1,0:T(8,128)} %shard_map.64.arrived), custom_call_target="tpu_custom_call" | custom-call | tf_op jit(solution)/shard_map/pallas_call | solution.py:620

commit v2 on v1

--- a/solution.py
+++ b/solution.py
@@ -242,30 +242,35 @@
         part = pl.ds(4 * q, 4)
 
         def send_all(half):
+            place = landed.at[q, :, me % HALF, pl.ds(4 * half, 4), :]
+
+            def source(there):
+                return packed.at[there // 2, there % 2, :, part, :]
+
+            def send(there):
+                pltpu.make_async_remote_copy(
+                    src_ref=source(there),
+                    dst_ref=place,
+                    send_sem=fwd_send,
+                    recv_sem=fwd_recv.at[q],
+                    device_id=(band, owner_of(there)),
+                    device_id_type=MESH,
+                ).start()
+
             def one(i, carry):
-                there = first + (turn + 1 + i) % number
-                target = owner_of(there)
-                source = packed.at[there // 2, there % 2, :, part, :]
-                place = landed.at[q, :, me % HALF, pl.ds(4 * half, 4), :]
-
-                @pl.when(target != me)
-                def _():
-                    pltpu.make_async_remote_copy(
-                        src_ref=source,
-                        dst_ref=place,
-                        send_sem=fwd_send,
-                        recv_sem=fwd_recv.at[q],
-                        device_id=(band, target),
-                        device_id_type=MESH,
-                    ).start()
-
-                @pl.when(target == me)
-                def _():
-                    pltpu.make_async_copy(source, place, fwd_recv.at[q]).start()
-
+                send(first + (turn + 1 + i) % number)
                 return carry
 
-            lax.fori_loop(0, number, one, 0)
+            lax.fori_loop(0, number - 1, one, 0)
+            last = first + turn % number
+
+            @pl.when(last != turn)
+            def _():
+                send(last)
+
+            @pl.when(last == turn)
+            def _():
+                pltpu.make_async_copy(source(turn), place, fwd_recv.at[q]).start()
 
         for half in range(2):
 
@@ -273,8 +278,9 @@
             def _():
                 send_all(half)
 
+    dispatch(0, 0, 16)
     forecast_row(2, band, state, halo.at[0], halo.at[1], kappa, packed)
-    dispatch(0, 0, 32)
+    dispatch(0, 16, 16)
     dispatch(1, 0, 32)
 
     obs_owner = owner_of(turn_of_pair(me))
@@ -471,16 +477,19 @@
         for v in range(3):
             reply[q, v] = updated[:, v * 128 : (v + 1) * 128].reshape(HALF, 8, 128)
 
+        place = returned.at[turn // 2, turn % 2, :, pl.ds(4 * q, 4), :]
+
+        def source(target, half):
+            return reply.at[q, :, target % HALF, pl.ds(4 * half, 4), :]
+
         def answer(i, carry):
             target = (me + 1 + i) % N_MEM
-            place = returned.at[turn // 2, turn % 2, :, pl.ds(4 * q, 4), :]
             for half in range(2):
-                source = reply.at[q, :, target % HALF, pl.ds(4 * half, 4), :]
-
-                @pl.when((target != me) & (target // HALF == half))
+
+                @pl.when(target // HALF == half)
                 def _():
                     pltpu.make_async_remote_copy(
-                        src_ref=source,
+                        src_ref=source(target, half),
                         dst_ref=place,
                         send_sem=back_send,
                         recv_sem=back_recv,
@@ -488,13 +497,14 @@
                         device_id_type=MESH,
                     ).start()
 
-                @pl.when((target == me) & (target // HALF == half))
-                def _():
-                    pltpu.make_async_copy(source, place, back_recv).start()
-
             return carry
 
-        lax.fori_loop(0, N_MEM, answer, 0)
+        lax.fori_loop(0, N_MEM - 1, answer, 0)
+        for half in range(2):
+
+            @pl.when(me // HALF == half)
+            def _():
+                pltpu.make_async_copy(source(me, half), place, back_recv).start()
 
     @pl.when(pair < N_MEM - 1)
     def _():

time: 63.2 us -> 62.7 us (level)
  no operation moved by 1% of the time
where the time goes in v2:
time: 62.7 us; the launch traced here: 62.5 us
  Pallas kernels  62.5 us (100%)
    pallas_call x1, Pallas kernels, body(): pl.pallas_call(kernel, out_shape=jax.ShapeDtypeStruct(half, F32), in_spec...  59.6 us
    pallas_call x1, Pallas kernels, body(): pl.pallas_call(unpack, out_shape=jax.ShapeDtypeStruct((3, 2, 2, 4, ROWS *...  2.9 us

profile of v2, /device:TPU:1, one launch (start us, length us, event | category | flops | bytes accessed | tf_op | source)
XLA Modules:
  0.0 62.5 jit_solution(12013310075282424506)
XLA Ops:
  0.0 59.6 %shard_map.64.arrived = f32[32,2,3,8,128]{4,3,2,1,0:T(8,128)} custom-call(f32[3,2,2,4,4096]{4,3,2,1,0:T(4,128)} %bitcast.10, f32[1,4096]{1,0:T(1,128)} %bitcast.11, s32[2,128]{1,0:T(2,128)} %bitcast.12, f32[2,128]{1,0:T(2,128)} %bitcast.13, f32[2,128]{1,0:T(2,128)} %bitcast.14, s32[2]{0:T(128)} %count.1), custom_call_target="tpu_custom_call" | custom-call | tf_op jit(solution)/shard_map/pallas_call | solution.py:582
  59.6 2.9 %shard_map.65 = f32[3,2,2,4,4096]{4,3,2,1,0:T(4,128)} custom-call(f32[32,2,3,8,128]{4,3,2,1,0:T(8,128)} %shard_map.64.arrived), custom_call_target="tpu_custom_call" | custom-call | tf_op jit(solution)/shard_map/pallas_call | solution.py:630

commit v3 on v2

--- a/solution.py
+++ b/solution.py
@@ -441,15 +441,18 @@
     def under(*pieces):
         return tuple(jnp.concatenate(x, axis=0) for x in zip(*pieces))
 
-    def analyse(q):
+    def gram_of(q, lanes):
+        left = (stack_high[q, :, lanes], stack_low[q, :, lanes])
+        return product(left, (top(left[0]), top(left[1])), transposed=True)
+
+    def analyse(q, own_gram):
         lanes = pl.ds(2 * q * SLOTS, SLOTS)
         high, small = split(side_in[q])
         rest = jnp.zeros((8, SLOTS), BF16)
         stack_high[q, pl.ds(0, 272), lanes] = jnp.concatenate([high, rest], axis=0)
         stack_low[q, pl.ds(0, 272), lanes] = jnp.concatenate([small, rest], axis=0)
 
-        left = (stack_high[q], stack_low[q])
-        gram = product(left, (top(left[0]), top(left[1])), transposed=True)
+        gram = own_gram + gram_of(q, lanes)
         force = split(gram[SAMPLE_TOTAL:])
         gram = top(gram) + identity(SAMPLE_TOTAL - 1.0)
         frobenius = jnp.sqrt(
@@ -506,17 +509,20 @@
             def _():
                 pltpu.make_async_copy(source(me, half), place, back_recv).start()
 
+    own_gram = gram_of(1, pl.ds(0, 2 * SLOTS))
+
     @pl.when(pair < N_MEM - 1)
     def _():
         to_left.wait_recv()
 
-    analyse(1)
+    analyse(1, own_gram)
+    own_gram = gram_of(0, pl.ds(SLOTS, 2 * SLOTS))
 
     @pl.when(pair > 0)
     def _():
         to_right.wait_recv()
 
-    analyse(0)
+    analyse(0, own_gram)
 
     pltpu.make_async_copy(returned, returned, back_recv).wait()
 

time: 62.7 us -> 62.6 us (level)
  no operation moved by 1% of the time
where the time goes in v3:
time: 62.6 us; the launch traced here: 62.4 us
  Pallas kernels  62.4 us (100%)
    pallas_call x1, Pallas kernels, body(): pl.pallas_call(kernel, out_shape=jax.ShapeDtypeStruct(half, F32), in_spec...  59.5 us
    pallas_call x1, Pallas kernels, body(): pl.pallas_call(unpack, out_shape=jax.ShapeDtypeStruct((3, 2, 2, 4, ROWS *...  2.9 us

profile of v3, /device:TPU:1, one launch (start us, length us, event | category | flops | bytes accessed | tf_op | source)
XLA Modules:
  0.0 62.4 jit_solution(12168748447911820909)
XLA Ops:
  0.0 59.5 %shard_map.64.arrived = f32[32,2,3,8,128]{4,3,2,1,0:T(8,128)} custom-call(f32[3,2,2,4,4096]{4,3,2,1,0:T(4,128)} %bitcast.10, f32[1,4096]{1,0:T(1,128)} %bitcast.11, s32[2,128]{1,0:T(2,128)} %bitcast.12, f32[2,128]{1,0:T(2,128)} %bitcast.13, f32[2,128]{1,0:T(2,128)} %bitcast.14, s32[2]{0:T(128)} %count.1), custom_call_target="tpu_custom_call" | custom-call | tf_op jit(solution)/shard_map/pallas_call | solution.py:588
  59.5 2.9 %shard_map.65 = f32[3,2,2,4,4096]{4,3,2,1,0:T(4,128)} custom-call(f32[32,2,3,8,128]{4,3,2,1,0:T(8,128)} %shard_map.64.arrived), custom_call_target="tpu_custom_call" | custom-call | tf_op jit(solution)/shard_map/pallas_call | solution.py:636
